TPU v7x, 32 devices: a whole 2x2x4 slice. The times are simulated.
32 devices in a mesh: user: 8 (over z, y), feat: 4 (over x, core).
Axes of the slice: x: 2, y: 2, z: 4, core: 2. Of those that a mesh axis runs over, the one named last changes fastest.
Arguments:
- view_one: bfloat16 [1024, 2048], P('user', 'feat'), may hold values from -8 to 8
- view_two: bfloat16 [1024, 2048], P('user', 'feat'), may hold values from -8 to 8
- partner: int32 [1024], P('user'), may hold values from 0 to 1023, each once
Outputs:
- grad_one: float32 [1024, 2048], P('user', 'feat')
- grad_two: float32 [1024, 2048], P('user', 'feat')
Inputs may be any that keep to these rules, and one draw needn't show every extreme that they name: `partner`: each index of view_two appears exactly once.
All inputs are finite; a program needn't handle non-finite values.
Results may differ from a plain program's by a relative error of at most 0.0028.
Values may be sent and summed in bfloat16 or wider, within the bound.
A program may use at most 128 MiB of HBM per device.

v0:
```python
import math

import jax
import jax.numpy as jnp
from jax import lax
from jax.sharding import PartitionSpec as P

D = 2048


def combined_all(value, axis, join):
    pieces = jax.tree.map(lambda part: lax.all_gather(part, axis), value)
    head = jax.tree.map(lambda part: part[0], pieces)
    tail = jax.tree.map(lambda part: part[1:], pieces)
    total, _ = lax.scan(lambda total, piece: (join(total, piece), None), head, tail)
    return total


def merge_stats(first, second):
    highest = jnp.maximum(first[0], second[0])
    return (
        highest,
        first[1] * jnp.exp(first[0] - highest) + second[1] * jnp.exp(second[0] - highest),
    )


def couple(scores_cols, row_lse, col_lse, partner, column_index):
    positive_mask = (column_index[:, None] == partner[None, :]).astype(jnp.float32)
    both = jnp.exp(scores_cols - row_lse[None, :]) + jnp.exp(scores_cols - col_lse[:, None])
    return (0.5 * both - positive_mask).astype(jnp.bfloat16)


def column_local(scores_cols):
    col_highest = jnp.max(scores_cols, axis=1)
    col_total = jnp.sum(jnp.exp(scores_cols - col_highest[:, None]), axis=1)
    return (col_highest, col_total)


def row_local(scores_cols):
    row_highest = jnp.max(scores_cols, axis=0)
    row_total = jnp.sum(jnp.exp(scores_cols - row_highest[None, :]), axis=0)
    return (row_highest, row_total)


def on_device(view_one, view_two, partner):
    logit_scale = 2.0 / math.sqrt(D)
    contract_width = (((1,), (1,)), ((), ()))
    contract_rows = (((0,), (0,)), ((), ()))
    every_two = lax.all_gather(view_two, "user", axis=0, tiled=True)
    block_rows = every_two
    scores_cols = lax.psum_scatter(
        logit_scale
        * lax.dot_general(block_rows, view_one, contract_width, preferred_element_type=jnp.float32),
        "feat",
        scatter_dimension=0,
        tiled=True,
    )
    row_highest, row_total = row_local(scores_cols)
    row_highest, row_total = combined_all((row_highest, row_total), "feat", merge_stats)
    col_highest, col_total = column_local(scores_cols)
    col_highest, col_total = combined_all((col_highest, col_total), "user", merge_stats)
    row_lse = row_highest + jnp.log(row_total)
    col_lse = col_highest + jnp.log(col_total)
    column_index = lax.axis_index("feat") * scores_cols.shape[0] + jnp.arange(
        scores_cols.shape[0], dtype=jnp.int32
    )
    coupling_local = couple(scores_cols, row_lse, col_lse, partner, column_index)
    coupling_all = lax.all_gather(coupling_local, "feat", axis=0, tiled=True)
    grad_one = lax.dot_general(
        coupling_all, every_two, contract_rows, preferred_element_type=jnp.float32
    )
    block_rows = coupling_all
    grad_two = lax.psum_scatter(
        jnp.dot(block_rows, view_one, preferred_element_type=jnp.float32),
        "user",
        scatter_dimension=0,
        tiled=True,
    )
    return (grad_one, grad_two)


def solution(mesh):
    return jax.shard_map(
        on_device,
        mesh=mesh,
        in_specs=(P("user", "feat"), P("user", "feat"), P("user")),
        out_specs=(P("user", "feat"), P("user", "feat")),
        check_vma=False,
    )
```

profile of v0, /device:TPU:0, one launch (start us, length us, event | category | flops | bytes accessed | tf_op | source)
XLA Modules:
  0.0 206.4 jit_solution(14852304024446860223)
XLA Ops:
  7.2 0.0 copy-start
  7.2 0.0 copy-start.2
  7.2 0.0 all-gather.10.cloned.1.call-start
  7.2 0.7 all-gather.10.cloned.1.call-update
  7.9 0.0 reduce-scatter.3.cloned.1.call-start
  8.0 45.1 %all-gather.10.cloned.1.call-done = bf16[1024,512]{1,0:T(8,128)(2,1)} async-done(((bf16[128,512]{1,0:T(8,128)(2,1)}), bf16[1024,512]{1,0:T(8,128)(2,1)}) %all-gather.10.cloned.1.call-update) | async-done | bytes 1048592 | tf_op jit(solution)/shard_map/all_gather | solution.py:49
  53.0 2.4 %convolution_multiply_fusion = f32[1024,128]{1,0:T(8,128)} fusion(bf16[1024,512]{1,0:T(8,128)(2,1)} %all-gather.10.cloned.1.call-done, bf16[128,512]{1,0:T(8,128)(2,1)S(1)} %copy-done), kind=kOutput, calls=%fused_computation.10 | convolution fusion | flops 134348800 | bytes 1703936 | tf_op jit(solution)/shard_map/dot_general | solution.py:53
  55.5 0.0 reduce-scatter.3.cloned.1.call-update
  55.5 0.0 reduce-scatter.5.cloned.1.call-start
  55.6 20.5 %reduce-scatter.3.cloned.1.call-done = f32[256,128]{1,0:T(8,128)} async-done(((f32[1024,128]{1,0:T(8,128)}), f32[256,128]{1,0:T(8,128)}) %reduce-scatter.3.cloned.1.call-update) | async-done | bytes 131088 | tf_op jit(solution)/shard_map/reduce_scatter | solution.py:51
  76.0 1.0 fusion.5
  77.1 1.1 exponential_reduce_fusion.1
  78.1 5.0 %all-gather.5 = f32[4,1,128]{2,1,0:T(1,128)S(1)} all-gather(f32[1,1,128]{2,1,0:T(1,128)S(1)} %bitcast.60), channel_id=3, replica_groups=mesh['user'=8,'feat'=4] {'feat'}, dimensions={0}, use_global_device_ids=true | all-gather | bytes 2560 | tf_op jit(solution)/shard_map/all_gather | solution.py:12
  83.2 5.0 %all-gather.4 = f32[4,1,128]{2,1,0:T(1,128)S(1)} all-gather(f32[1,1,128]{2,1,0:T(1,128)S(1)} %bitcast.58), channel_id=2, replica_groups=mesh['user'=8,'feat'=4] {'feat'}, dimensions={0}, use_global_device_ids=true | all-gather | bytes 2560 | tf_op jit(solution)/shard_map/all_gather | solution.py:12
  88.2 20.5 %all-gather.7 = f32[8,1,256]{2,1,0:T(1,128)S(1)} all-gather(f32[1,1,256]{2,1,0:T(1,128)S(1)} %bitcast.59), channel_id=5, replica_groups=mesh['user'=8,'feat'=4] {'user'}, dimensions={0}, use_global_device_ids=true | all-gather | bytes 9216 | tf_op jit(solution)/shard_map/all_gather | solution.py:12
  108.7 16.3 %all-gather.6 = f32[8,1,256]{2,1,0:T(1,128)S(1)} all-gather(f32[1,1,256]{2,1,0:T(1,128)S(1)} %bitcast.57), channel_id=4, replica_groups=mesh['user'=8,'feat'=4] {'user'}, dimensions={0}, use_global_device_ids=true | all-gather | bytes 9216 | tf_op jit(solution)/shard_map/all_gather | solution.py:12
  125.0 0.1 while.24
  125.1 0.3 while.25
  125.5 1.0 subtract_convert_fusion
  126.6 5.8 %all_gather.39 = bf16[1024,128]{1,0:T(8,128)(2,1)S(1)} all-gather(bf16[256,128]{1,0:T(8,128)(2,1)S(1)} %subtract_convert_fusion), channel_id=1, replica_groups=mesh['user'=8,'feat'=4] {'feat'}, dimensions={0}, use_global_device_ids=true | all-gather | bytes 327680 | tf_op jit(solution)/shard_map/all_gather | solution.py:68
  132.4 1.8 fusion.8
  134.1 0.0 reduce-scatter.5.cloned.1.call-update
  134.2 1.0 fusion.7
  135.2 64.7 %reduce-scatter.5.cloned.1.call-done = f32[128,512]{1,0:T(8,128)} async-done(((f32[1024,512]{1,0:T(8,128)}), f32[128,512]{1,0:T(8,128)}) %reduce-scatter.5.cloned.1.call-update) | async-done | bytes 262160 | tf_op jit(solution)/shard_map/reduce_scatter | solution.py:73
  (36 shorter events, 0.3 us)
Async XLA Ops:
  7.2 45.9 %copy-start = (bf16[128,512]{1,0:T(8,128)(2,1)S(1)}, bf16[128,512]{1,0:T(8,128)(2,1)}, u32[]{:S(2)}) copy-start(bf16[128,512]{1,0:T(8,128)(2,1)} %param.7) | copy-start | bytes 393220
  7.2 118.4 %copy-start.2 = (s32[128]{0:T(128)S(1)}, s32[128]{0:T(128)}, u32[]{:S(2)}) copy-start(s32[128]{0:T(128)} %param.9) | copy-start | bytes 1540
  7.2 45.8 %all-gather.10.cloned.1.call-start = ((), (), s32[]{:S(2)}) async-start(), calls=%async_computation.2 | async-start | bytes 1179648 | tf_op jit(solution)/shard_map/all_gather | solution.py:49
  7.9 68.1 %reduce-scatter.3.cloned.1.call-start = ((), (), s32[]{:S(2)}) async-start(), calls=%async_computation.3 | async-start | bytes 655360 | tf_op jit(solution)/shard_map/reduce_scatter | solution.py:51
  55.5 144.4 %reduce-scatter.5.cloned.1.call-start = ((), (), s32[]{:S(2)}) async-start(), calls=%async_computation.4 | async-start | bytes 2359296 | tf_op jit(solution)/shard_map/reduce_scatter | solution.py:73
  132.4 1.8 copy-start.1
Sparse Core Ops, SparseCore 0:
  10.1 42.8 all-gather.9
  55.6 20.3 reduce-scatter.2
  134.3 65.5 reduce-scatter.4
where the time goes:
time: 207 us; the launch traced here: 206 us
  waiting for transfers between devices  131 us (63%)
  blocking collectives  52.6 us (25%)
  between operations  13.9 us (7%)
  matrix products  5.23 us (3%)
  other arithmetic  3.38 us (2%)
    reduce_scatter x1, waiting for transfers between devices, on_device(): lax.psum_scatter(jnp.dot(block_rows, view_one, preferred_element_type=jnp...  64.7 us
    all_gather x4, blocking collectives, combined_all(): pieces = jax.tree.map(lambda part: lax.all_gather(part, axis), value)  46.8 us
    all_gather x1, waiting for transfers between devices, on_device(): every_two = lax.all_gather(view_two, 'user', axis=0, tiled=True)  45.1 us
    reduce_scatter x1, waiting for transfers between devices, on_device(): lax.psum_scatter(logit_scale * lax.dot_general(block_rows, view_one, cont...  20.5 us
    all_gather x1, blocking collectives, on_device(): coupling_all = lax.all_gather(coupling_local, 'feat', axis=0, tiled=True)  5.79 us
  transfers between devices with their start and end apart: 3, of which 3 were waited for; matrix products, arithmetic and copies ran while one was open for 1% of the time, Pallas kernels for 0%

commit v1 on v0

v1 whole, which is shorter than its diff:
```python
import functools
import math

import jax
import jax.numpy as jnp
from jax import lax
from jax.experimental import pallas as pl
from jax.experimental.pallas import tpu as pltpu
from jax.sharding import PartitionSpec as P

D = 2048
MESH = pl.DeviceIdType.MESH
NT = (((1,), (1,)), ((), ()))
TN = (((0,), (0,)), ((), ()))


def line_length(users):
    length = 1
    while length * length < users:
        length *= 2
    return length


def kernel(users, feats, one_ref, two_ref, partner_ref, g1_ref, g2_ref,
           views, part, rs, colst, rowst, coup, cols,
           local_sem, view_recv, line_send, group_send, rs_send, rs_recv,
           col_send, col_recv, row_send, row_recv, coup_send, coup_recv,
           turn_send, turn_recv, cols_send, cols_recv):
    rows, width = one_ref.shape
    quarter = rows // feats
    length = line_length(users)
    group = users // length
    scale = 2.0 / math.sqrt(D)
    u = lax.axis_index("user")
    f = lax.axis_index("feat")
    z = u // group
    y = lax.rem(u, group)
    mine = pl.ds(pl.multiple_of(f * quarter, quarter), quarter)

    loads = [pltpu.make_async_copy(ref, views.at[v, u], local_sem.at[v])
             for v, ref in enumerate((two_ref, one_ref))]
    for load in loads:
        load.start()

    def user_at(k):
        return lax.rem(u + k, users)

    def feat_at(k):
        return lax.rem(f + k, feats)

    barrier = pltpu.get_barrier_semaphore()
    for k in range(1, users):
        pl.semaphore_signal(barrier, inc=1, device_id=(user_at(k), f), device_id_type=MESH)
    for k in range(1, feats):
        pl.semaphore_signal(barrier, inc=1, device_id=(u, feat_at(k)), device_id_type=MESH)
    pl.semaphore_wait(barrier, users + feats - 2)

    def remote(src, dst, send, recv, user, feat):
        return pltpu.make_async_remote_copy(
            src_ref=src, dst_ref=dst, send_sem=send, recv_sem=recv,
            device_id=(user, feat), device_id_type=MESH)

    def along(v, b, step):
        return remote(views.at[v, b], views.at[v, b], line_send.at[v, b, (step + 1) // 2],
                      view_recv.at[v, b], u + step * group, f)

    def across(v, b, k):
        return remote(views.at[v, b], views.at[v, b], group_send.at[v, b, k - 1],
                      view_recv.at[v, b], z * group + lax.rem(y + k, group), f)

    def arrived(v, b):
        across(v, b, 1).wait_recv()

    def each_on_line(d, body):
        for step in ((1, -1) if d else (0,)):
            src = z + step * d

            @pl.when((src >= 0) & (src < length))
            def _():
                body(src, step)

    def onward(src, step, act):
        for way in ((-step,) if step else (1, -1)):
            @pl.when((z + way >= 0) & (z + way < length))
            def _():
                act(way)

    def pass_on(v, d):
        def body(src, step):
            b = src * group + y
            if d:
                arrived(v, b)
            onward(src, step, lambda way: along(v, b, way).start())
            for k in range(1, group):
                across(v, b, k).start()
        each_on_line(d, body)

    def sent(v):
        for d in range(length):
            def body(src, step):
                b = src * group + y
                onward(src, step, lambda way: along(v, b, way).wait_send())
                for k in range(1, group):
                    across(v, b, k).wait_send()
            each_on_line(d, body)

    def rs_copy(b, k):
        to = feat_at(k)
        return remote(part.at[b, pl.ds(pl.multiple_of(to * quarter, quarter), quarter)], rs.at[k - 1, b],
                      rs_send.at[k - 1, b], rs_recv.at[k - 1, b], u, to)

    def score(b):
        part[b] = lax.dot_general(views[0, b], views[1, u], NT, preferred_element_type=jnp.float32)
        for k in range(1, feats):
            rs_copy(b, k).start()

    def score_line(d):
        each_on_line(d, lambda src, step: score(src * group + y))

    def score_group(d):
        def body(src, step):
            def one(k, carry):
                b = src * group + lax.rem(y + k, group)
                arrived(0, b)
                score(b)
                return carry
            lax.fori_loop(1, group, one, 0)
        each_on_line(d, body)

    loads[0].wait()
    pass_on(0, 0)
    loads[1].wait()
    score_line(0)
    for d in range(1, length):
        pass_on(0, d)
        score_line(d)
        score_group(d - 1)
    pass_on(1, 0)
    score_group(length - 1)

    def rs_wait(b, carry):
        for k in range(1, feats):
            rs_copy(b, k).wait_recv()
        return carry
    lax.fori_loop(0, users, rs_wait, 0)
    total = part[:, mine, :]
    for k in range(feats - 1):
        total = total + rs[k]
    scores = (scale * total).reshape(users * quarter, rows)
    scores_t = scores.T

    row_high = jnp.max(scores, axis=0, keepdims=True)
    rowst[f, 0:1] = row_high
    rowst[f, 1:2] = jnp.sum(jnp.exp(scores - row_high), axis=0, keepdims=True)
    col_high = jnp.max(scores_t, axis=0, keepdims=True)
    colst[u, 0:1] = col_high
    colst[u, 1:2] = jnp.sum(jnp.exp(scores_t - col_high), axis=0, keepdims=True)

    def col_copy(k):
        return remote(colst.at[u], colst.at[u], col_send.at[k - 1], col_recv.at[k - 1], user_at(k), f)

    def row_copy(k):
        return remote(rowst.at[f], rowst.at[f], row_send.at[k - 1], row_recv.at[k - 1], u, feat_at(k))

    for k in range(1, users):
        col_copy(k).start()
    for k in range(1, feats):
        row_copy(k).start()
    pass_on(1, 1)
    for k in range(1, feats):
        row_copy(k).wait_recv()
    for k in range(1, users):
        col_copy(k).wait_recv()

    def merged(stats, count):
        high = stats[0, 0:1]
        for k in range(1, count):
            high = jnp.maximum(high, stats[k, 0:1])
        whole = jnp.zeros_like(high)
        for k in range(count):
            whole = whole + stats[k, 1:2] * jnp.exp(stats[k, 0:1] - high)
        return high + jnp.log(whole)

    row_lse = merged(rowst, feats)
    col_lse = merged(colst, users)
    both = jnp.exp(scores - row_lse) + jnp.exp(scores_t - col_lse).T
    block = (users, quarter, rows)
    index = (lax.broadcasted_iota(jnp.int32, block, 0) * rows
             + lax.broadcasted_iota(jnp.int32, block, 1) + f * quarter)
    hit = jnp.where(index == partner_ref[...].reshape(1, 1, rows), 1.0, 0.0)
    coupling = (0.5 * both.reshape(block) - hit).astype(jnp.bfloat16)
    coup[:, mine, :] = coupling

    def turn_copy(k):
        return remote(coup.at[user_at(k), mine], cols.at[u, mine],
                      turn_send.at[k - 1], turn_recv.at[k - 1], user_at(k), f)

    def coup_copy(k):
        return remote(coup.at[:, mine], coup.at[:, mine],
                      coup_send.at[k - 1], coup_recv.at[k - 1], u, feat_at(k))

    def cols_copy(k):
        return remote(cols.at[:, mine], cols.at[:, mine],
                      cols_send.at[k - 1], cols_recv.at[k - 1], u, feat_at(k))

    for k in range(1, users):
        turn_copy(k).start()
    for k in range(1, feats):
        coup_copy(k).start()
    cols[u, mine, :] = coup[u, mine, :]
    for d in range(2, length):
        pass_on(1, d)
    for k in range(1, users):
        turn_copy(k).wait_recv()
    for k in range(1, feats):
        cols_copy(k).start()

    def summed(out_ref, term):
        out_ref[...] = term(0)
        if users <= 8:
            for b in range(1, users):
                out_ref[...] += term(b)
        else:
            def step(b, carry):
                out_ref[...] += term(b)
                return carry
            lax.fori_loop(1, users, step, 0)

    for k in range(1, feats):
        coup_copy(k).wait_recv()
    summed(g1_ref, lambda b: lax.dot_general(coup[b], views[0, b], TN, preferred_element_type=jnp.float32))

    for d in range(length):
        def rest(src, step):
            def one(k, carry):
                arrived(1, src * group + lax.rem(y + k, group))
                return carry
            lax.fori_loop(1, group, one, 0)
        each_on_line(d, rest)
    for k in range(1, feats):
        cols_copy(k).wait_recv()
    summed(g2_ref, lambda b: jnp.dot(cols[b], views[1, b], preferred_element_type=jnp.float32))

    sent(0)
    sent(1)

    def rs_sent(b, carry):
        for k in range(1, feats):
            rs_copy(b, k).wait_send()
        return carry
    lax.fori_loop(0, users, rs_sent, 0)
    for k in range(1, users):
        col_copy(k).wait_send()
        turn_copy(k).wait_send()
    for k in range(1, feats):
        row_copy(k).wait_send()
        coup_copy(k).wait_send()
        cols_copy(k).wait_send()


def on_device(users, feats, view_one, view_two, partner):
    rows, width = view_one.shape
    quarter = rows // feats
    group = users // line_length(users)
    out = jax.ShapeDtypeStruct((rows, width), jnp.float32)
    vmem = pl.BlockSpec(memory_space=pltpu.VMEM)
    anywhere = pl.BlockSpec(memory_space=pl.ANY)
    dma = pltpu.SemaphoreType.DMA
    f32, bf16 = jnp.float32, jnp.bfloat16
    return pl.pallas_call(
        functools.partial(kernel, users, feats),
        out_shape=(out, out),
        in_specs=[anywhere, anywhere, vmem],
        out_specs=(vmem, vmem),
        scratch_shapes=[
            pltpu.VMEM((2, users, rows, width), bf16),
            pltpu.VMEM((users, rows, rows), f32),
            pltpu.VMEM((feats - 1, users, quarter, rows), f32),
            pltpu.VMEM((users, 8, users * quarter), f32),
            pltpu.VMEM((feats, 8, rows), f32),
            pltpu.VMEM((users, rows, rows), bf16),
            pltpu.VMEM((users, rows, rows), bf16),
            dma((2,)),
            dma((2, users)),
            dma((2, users, 2)),
            dma((2, users, max(group - 1, 1))),
            dma((feats - 1, users)),
            dma((feats - 1, users)),
            dma((users - 1,)),
            dma((users - 1,)),
            dma((feats - 1,)),
            dma((feats - 1,)),
            dma((feats - 1,)),
            dma((feats - 1,)),
            dma((users - 1,)),
            dma((users - 1,)),
            dma((feats - 1,)),
            dma((feats - 1,)),
        ],
        compiler_params=pltpu.CompilerParams(
            collective_id=0, has_side_effects=True, vmem_limit_bytes=60 * 1024 * 1024),
        cost_estimate=pl.CostEstimate(
            flops=6 * users * rows * rows * width, bytes_accessed=16 * rows * width,
            transcendentals=4 * users * quarter * rows),
    )(view_one, view_two, partner.reshape(1, rows))


def solution(mesh):
    return jax.shard_map(
        functools.partial(on_device, mesh.shape["user"], mesh.shape["feat"]),
        mesh=mesh,
        in_specs=(P("user", "feat"), P("user", "feat"), P("user")),
        out_specs=(P("user", "feat"), P("user", "feat")),
        check_vma=False,
    )
```

time: 207 us -> 45.1 us (0.22)
  waiting for transfers between devices: 131 us -> 0 us
  blocking collectives: 52.6 us -> 0 us
  Pallas kernels: 0 us -> 41.9 us
  between operations: 13.9 us -> 0.65 us
  matrix products: 5.23 us -> 0 us
  other arithmetic: 3.38 us -> 0 us
  local copies, waits for them, and re-layouts: 0.1 us -> 2.42 us
    reduce_scatter x2 -> x0, waiting for transfers between devices: 85.1 us -> none  [the longest x1 64.7 us: on_device(): lax.psum_scatter(jnp.dot(block_rows, view_one, preferred_element_type=jnp...]
    all_gather x5 -> x0, blocking collectives: 52.6 us -> none  [the longest x4 46.8 us: combined_all(): pieces = jax.tree.map(lambda part: lax.all_gather(part, axis), value)]
    all_gather x1 -> x0, waiting for transfers between devices: 45.1 us -> none  [on_device(): every_two = lax.all_gather(view_two, 'user', axis=0, tiled=True)]
    pallas_call x0 -> x1, Pallas kernels: none -> 41.9 us  [on_device(): pl.pallas_call(functools.partial(kernel, users, feats), out_shape=(out, o...]
    dot_general x3 -> x0, matrix products: 5.23 us -> none  [the longest x1 2.44 us: on_device(): lax.dot_general(block_rows, view_one, contract_width, preferred_element_t...]
    unnamed x10 -> x4, local copies, waits for them, and re-layouts: 0.03 us -> 2.42 us
  transfers between devices with their start and end apart: 3 -> 0, of which waited for: 3 -> 0; matrix products, arithmetic and copies ran while one was open for 1% -> 0% of each run, Pallas kernels for 0% -> 0%
where the time goes in v1:
time: 45.1 us; the launch traced here: 44.9 us
  Pallas kernels  41.9 us (93%)
  local copies, waits for them, and re-layouts  2.42 us (5%)
  between operations  0.65 us (1%)
    pallas_call x1, Pallas kernels, on_device(): pl.pallas_call(functools.partial(kernel, users, feats), out_shape=(out, o...  41.9 us
    unnamed x4, local copies, waits for them, and re-layouts  2.42 us

profile of v1, /device:TPU:0, one launch (start us, length us, event | category | flops | bytes accessed | tf_op | source)
XLA Modules:
  0.0 44.9 jit_solution(77141676059569133)
XLA Ops:
  0.6 41.9 %shard_map.50 = (f32[128,512]{1,0:T(8,128)}, f32[128,512]{1,0:T(8,128)}) custom-call(bf16[128,512]{1,0:T(8,128)(2,1)} %one_ref.1, bf16[128,512]{1,0:T(8,128)(2,1)} %two_ref.1, s32[1,128]{1,0:T(1,128)} %bitcast.1), custom_call_target="tpu_custom_call" | custom-call | flops 402653184 | bytes 1048576 | tf_op jit(solution)/shard_map/pallas_call | solution.py:270
  42.5 0.0 copy-start
  42.5 1.7 %copy.7 = f32[128,512]{1,0:T(8,128)} copy(f32[128,512]{1,0:T(8,128)} %get-tuple-element.4) | data formatting | bytes 524288
  44.2 0.0 copy-done
  44.2 0.7 %copy.8 = f32[128,512]{1,0:T(8,128)} copy(f32[128,512]{1,0:T(8,128)S(1)} %copy-done) | data formatting | bytes 524288
Async XLA Ops:
  42.5 1.7 %copy-start = (f32[128,512]{1,0:T(8,128)S(1)}, f32[128,512]{1,0:T(8,128)}, u32[]{:S(2)}) copy-start(f32[128,512]{1,0:T(8,128)} %get-tuple-element.5) | copy-start | bytes 786436

commit v2 on v1

v2 whole, which is shorter than its diff:
```python
import functools
import math

import jax
import jax.numpy as jnp
from jax import lax
from jax.experimental import pallas as pl
from jax.experimental.pallas import tpu as pltpu
from jax.sharding import PartitionSpec as P

D = 2048
MESH = pl.DeviceIdType.MESH
NT = (((1,), (1,)), ((), ()))
TN = (((0,), (0,)), ((), ()))


def line_length(users):
    length = 1
    while length * length < users:
        length *= 2
    return length


def kernel(users, feats, one_ref, two_ref, partner_ref, g1_ref, g2_ref,
           views, partners, part, rs, colst, rowst, stage, coup, cols,
           local_sem, view_recv, line_send, group_send, partner_send, partner_recv,
           rs_send, rs_recv, col_send, col_recv, row_send, row_recv,
           coup_send, coup_recv, turn_send, turn_recv, cols_send, cols_recv):
    rows, width = one_ref.shape
    quarter = rows // feats
    length = line_length(users)
    group = users // length
    plane = group * feats
    scale = 2.0 / math.sqrt(D)
    u = lax.axis_index("user")
    f = lax.axis_index("feat")
    z = u // group
    y = lax.rem(u, group)
    mine = pl.ds(pl.multiple_of(f * quarter, quarter), quarter)

    loads = [pltpu.make_async_copy(ref, views.at[v, u], local_sem.at[v])
             for v, ref in enumerate((two_ref, one_ref))]
    for load in loads:
        load.start()
    partners[y] = partner_ref[...]

    def line_at(k):
        return lax.rem(z + k, length)

    def plane_at(p):
        return lax.rem(y + p // feats, group), lax.rem(f + p % feats, feats)

    barrier = pltpu.get_barrier_semaphore()
    for k in range(1, length):
        pl.semaphore_signal(barrier, inc=1, device_id=(line_at(k) * group + y, f), device_id_type=MESH)
    for p in range(1, plane):
        to_y, to_f = plane_at(p)
        pl.semaphore_signal(barrier, inc=1, device_id=(z * group + to_y, to_f), device_id_type=MESH)
    pl.semaphore_wait(barrier, length + plane - 2)

    def remote(src, dst, send, recv, to_z, to_y, to_f):
        return pltpu.make_async_remote_copy(
            src_ref=src, dst_ref=dst, send_sem=send, recv_sem=recv,
            device_id=(to_z * group + to_y, to_f), device_id_type=MESH)

    def along(v, src, step):
        b = src * group + y
        return remote(views.at[v, b], views.at[v, b], line_send.at[v, src, (step + 1) // 2],
                      view_recv.at[v, b], z + step, y, f)

    def across(v, src, k):
        b = src * group + y
        return remote(views.at[v, b], views.at[v, b], group_send.at[v, src, k - 1],
                      view_recv.at[v, b], z, lax.rem(y + k, group), f)

    def arrived(v, b):
        remote(views.at[v, b], views.at[v, b], line_send.at[v, 0, 0], view_recv.at[v, b], z, y, f).wait_recv()

    def each_on_line(d, body):
        for step in ((1, -1) if d else (0,)):
            src = z + step * d

            @pl.when((src >= 0) & (src < length))
            def _():
                body(src, step)

    def onward(step, act):
        for way in ((-step,) if step else (1, -1)):
            @pl.when((z + way >= 0) & (z + way < length))
            def _():
                act(way)

    def pass_on(v, d):
        def body(src, step):
            if d:
                arrived(v, src * group + y)
            onward(step, lambda way: along(v, src, way).start())
        each_on_line(d, body)

    def cross(v, d):
        def body(src, step):
            for k in range(1, group):
                across(v, src, k).start()
        each_on_line(d, body)

    def sent(v):
        for d in range(length):
            def body(src, step):
                onward(step, lambda way: along(v, src, way).wait_send())
                for k in range(1, group):
                    across(v, src, k).wait_send()
            each_on_line(d, body)

    def crossed(v):
        def one(src, carry):
            for k in range(1, group):
                arrived(v, src * group + lax.rem(y + k, group))
            return carry
        lax.fori_loop(0, length, one, 0)

    def partner_copy(k):
        return remote(partners.at[y], partners.at[y], partner_send.at[k - 1], partner_recv.at[k - 1],
                      z, lax.rem(y + k, group), f)

    def rs_copy(src, k):
        to = lax.rem(f + k, feats)
        return remote(part.at[src, pl.ds(pl.multiple_of(to * quarter, quarter), quarter)], rs.at[k - 1, src],
                      rs_send.at[k - 1, src], rs_recv.at[k - 1, src], z, y, to)

    def score(d):
        def body(src, step):
            part[src] = lax.dot_general(
                views[0, src * group + y], views[1, pl.ds(z * group, group)].reshape(group * rows, width),
                NT, preferred_element_type=jnp.float32)
            for k in range(1, feats):
                rs_copy(src, k).start()
        each_on_line(d, body)

    loads[0].wait()
    pass_on(0, 0)
    loads[1].wait()
    cross(1, 0)
    for k in range(1, group):
        partner_copy(k).start()
    cross(0, 0)
    for k in range(1, group):
        arrived(1, z * group + lax.rem(y + k, group))
    score(0)
    for d in range(1, length):
        pass_on(0, d)
        if d == length - 1:
            pass_on(1, 0)
        score(d)
        cross(0, d)

    def rs_wait(src, carry):
        for k in range(1, feats):
            rs_copy(src, k).wait_recv()
        return carry
    lax.fori_loop(0, length, rs_wait, 0)
    total = part[:, mine, :]
    for k in range(feats - 1):
        total = total + rs[k]
    scores = (scale * total).reshape(length * quarter, group * rows)
    scores_t = scores.T

    row_high = jnp.max(scores, axis=0, keepdims=True)
    row_exp = jnp.exp(scores - row_high)
    rowst[y, f, 0:1] = row_high
    rowst[y, f, 1:2] = jnp.sum(row_exp, axis=0, keepdims=True)
    col_high = jnp.max(scores_t, axis=0, keepdims=True)
    col_exp = jnp.exp(scores_t - col_high)
    colst[z, 0:1] = col_high
    colst[z, 1:2] = jnp.sum(col_exp, axis=0, keepdims=True)

    def col_copy(k):
        return remote(colst.at[z], colst.at[z], col_send.at[k - 1], col_recv.at[k - 1], line_at(k), y, f)

    def row_copy(p):
        return remote(rowst.at[y, f], rowst.at[y, f], row_send.at[p - 1], row_recv.at[p - 1], z, *plane_at(p))

    for k in range(1, length):
        col_copy(k).start()
    for p in range(1, plane):
        row_copy(p).start()
    pass_on(1, 1)
    cross(1, 1)
    for k in range(1, group):
        partner_copy(k).wait_recv()
    for p in range(1, plane):
        row_copy(p).wait_recv()
    for k in range(1, length):
        col_copy(k).wait_recv()

    def share(own, stats):
        high = functools.reduce(jnp.maximum, [highest for highest, _ in stats])
        whole = sum(value * jnp.exp(highest - high) for highest, value in stats)
        return 0.5 * jnp.exp(own - (high + jnp.log(whole)))

    row_share = share(row_high, [(rowst[i, j, 0:1], rowst[i, j, 1:2]) for i in range(group) for j in range(feats)])
    col_share = share(col_high, [(colst[i, 0:1], colst[i, 1:2]) for i in range(length)])
    both = row_exp * row_share + (col_exp * col_share).T
    block = (length, quarter, rows)
    index = (lax.broadcasted_iota(jnp.int32, block, 0) * (group * rows)
             + lax.broadcasted_iota(jnp.int32, block, 1) + (y * rows + f * quarter))
    for i in range(group):
        hit = jnp.where(index == partners[i].reshape(1, 1, rows), 1.0, 0.0)
        stage[i] = (both[:, i * rows:(i + 1) * rows].reshape(block) - hit).astype(jnp.bfloat16)

    def turn_copy(k):
        return remote(stage.at[:, line_at(k)], cols.at[pl.ds(z * group, group), mine],
                      turn_send.at[k - 1], turn_recv.at[k - 1], line_at(k), y, f)

    def coup_copy(p):
        to_y, to_f = plane_at(p)
        return remote(stage.at[to_y], coup.at[:, y, mine], coup_send.at[p - 1], coup_recv.at[p - 1], z, to_y, to_f)

    def cols_copy(k):
        return remote(cols.at[:, mine], cols.at[:, mine],
                      cols_send.at[k - 1], cols_recv.at[k - 1], z, y, lax.rem(f + k, feats))

    for k in range(1, length):
        turn_copy(k).start()
    for p in range(1, plane):
        coup_copy(p).start()
    coup[:, y, mine, :] = stage[y]
    cols[pl.ds(z * group, group), mine, :] = stage[:, z]
    pass_on(1, 2)
    cross(1, 2)
    for k in range(1, length):
        turn_copy(k).wait_recv()
    for k in range(1, feats):
        cols_copy(k).start()
    for d in range(3, length):
        pass_on(1, d)
        cross(1, d)

    def summed(out_ref, term):
        chunk = math.gcd(users, 8)
        out_ref[...] = term(0, chunk)

        def step(c, carry):
            out_ref[...] += term(c * chunk, chunk)
            return carry
        if users > chunk:
            lax.fori_loop(1, users // chunk, step, 0)

    def one_term(b, chunk):
        left = coup[pl.ds(b // group, chunk // group)].reshape(chunk * rows, rows)
        return lax.dot_general(left, views[0, pl.ds(b, chunk)].reshape(chunk * rows, width),
                               TN, preferred_element_type=jnp.float32)

    def two_term(b, chunk):
        left = jnp.concatenate([cols[b + i] for i in range(chunk)], axis=1)
        return jnp.dot(left, views[1, pl.ds(b, chunk)].reshape(chunk * rows, width),
                       preferred_element_type=jnp.float32)

    for p in range(1, plane):
        coup_copy(p).wait_recv()
    crossed(0)
    summed(g1_ref, one_term)

    def late(src, carry):
        @pl.when(src != z)
        def _():
            for k in range(1, group):
                arrived(1, src * group + lax.rem(y + k, group))
        return carry
    lax.fori_loop(0, length, late, 0)
    for k in range(1, feats):
        cols_copy(k).wait_recv()
    summed(g2_ref, two_term)

    sent(0)
    sent(1)

    def rs_sent(src, carry):
        for k in range(1, feats):
            rs_copy(src, k).wait_send()
        return carry
    lax.fori_loop(0, length, rs_sent, 0)
    for k in range(1, group):
        partner_copy(k).wait_send()
    for k in range(1, length):
        col_copy(k).wait_send()
        turn_copy(k).wait_send()
    for p in range(1, plane):
        row_copy(p).wait_send()
        coup_copy(p).wait_send()
    for k in range(1, feats):
        cols_copy(k).wait_send()


def on_device(users, feats, view_one, view_two, partner):
    rows, width = view_one.shape
    quarter = rows // feats
    length = line_length(users)
    group = users // length
    plane = group * feats
    out = jax.ShapeDtypeStruct((rows, width), jnp.float32)
    vmem = pl.BlockSpec(memory_space=pltpu.VMEM)
    anywhere = pl.BlockSpec(memory_space=pl.ANY)
    dma = pltpu.SemaphoreType.DMA
    f32, bf16 = jnp.float32, jnp.bfloat16
    return pl.pallas_call(
        functools.partial(kernel, users, feats),
        out_shape=(out, out),
        in_specs=[anywhere, anywhere, vmem],
        out_specs=(vmem, vmem),
        scratch_shapes=[
            pltpu.VMEM((2, users, rows, width), bf16),
            pltpu.VMEM((group, 1, rows), jnp.int32),
            pltpu.VMEM((length, rows, group * rows), f32),
            pltpu.VMEM((feats - 1, length, quarter, group * rows), f32),
            pltpu.VMEM((length, 8, length * quarter), f32),
            pltpu.VMEM((group, feats, 8, group * rows), f32),
            pltpu.VMEM((group, length, quarter, rows), bf16),
            pltpu.VMEM((length, group, rows, rows), bf16),
            pltpu.VMEM((users, rows, rows), bf16),
            dma((2,)),
            dma((2, users)),
            dma((2, length, 2)),
            dma((2, length, group - 1)),
            dma((group - 1,)), dma((group - 1,)),
            dma((feats - 1, length)), dma((feats - 1, length)),
            dma((length - 1,)), dma((length - 1,)),
            dma((plane - 1,)), dma((plane - 1,)),
            dma((plane - 1,)), dma((plane - 1,)),
            dma((length - 1,)), dma((length - 1,)),
            dma((feats - 1,)), dma((feats - 1,)),
        ],
        compiler_params=pltpu.CompilerParams(
            collective_id=0, has_side_effects=True, vmem_limit_bytes=60 * 1024 * 1024),
        cost_estimate=pl.CostEstimate(
            flops=6 * users * rows * rows * width, bytes_accessed=16 * rows * width,
            transcendentals=4 * users * quarter * rows),
    )(view_one, view_two, partner.reshape(1, rows))


def solution(mesh):
    return jax.shard_map(
        functools.partial(on_device, mesh.shape["user"], mesh.shape["feat"]),
        mesh=mesh,
        in_specs=(P("user", "feat"), P("user", "feat"), P("user")),
        out_specs=(P("user", "feat"), P("user", "feat")),
        check_vma=False,
    )
```

time: 45.1 us -> 43.2 us (0.958)
  Pallas kernels: 41.9 us -> 40 us
    pallas_call x1, Pallas kernels: 41.9 us -> 40 us  [on_device(): pl.pallas_call(functools.partial(kernel, users, feats), out_shape=(out, o...]
where the time goes in v2:
time: 43.2 us; the launch traced here: 43 us
  Pallas kernels  40 us (93%)
  local copies, waits for them, and re-layouts  2.42 us (6%)
  between operations  0.65 us (2%)
    pallas_call x1, Pallas kernels, on_device(): pl.pallas_call(functools.partial(kernel, users, feats), out_shape=(out, o...  40 us
    unnamed x4, local copies, waits for them, and re-layouts  2.42 us

profile of v2, /device:TPU:0, one launch (start us, length us, event | category | flops | bytes accessed | tf_op | source)
XLA Modules:
  0.0 43.0 jit_solution(9580154679432358753)
XLA Ops:
  0.6 40.0 %shard_map.50 = (f32[128,512]{1,0:T(8,128)}, f32[128,512]{1,0:T(8,128)}) custom-call(bf16[128,512]{1,0:T(8,128)(2,1)} %one_ref.1, bf16[128,512]{1,0:T(8,128)(2,1)} %two_ref.1, s32[1,128]{1,0:T(1,128)} %bitcast.1), custom_call_target="tpu_custom_call" | custom-call | flops 402653184 | bytes 1048576 | tf_op jit(solution)/shard_map/pallas_call | solution.py:305
  40.6 0.0 copy-start
  40.6 1.7 %copy.7 = f32[128,512]{1,0:T(8,128)} copy(f32[128,512]{1,0:T(8,128)} %get-tuple-element.4) | data formatting | bytes 524288
  42.3 0.0 copy-done
  42.3 0.7 %copy.8 = f32[128,512]{1,0:T(8,128)} copy(f32[128,512]{1,0:T(8,128)S(1)} %copy-done) | data formatting | bytes 524288
Async XLA Ops:
  40.6 1.7 %copy-start = (f32[128,512]{1,0:T(8,128)S(1)}, f32[128,512]{1,0:T(8,128)}, u32[]{:S(2)}) copy-start(f32[128,512]{1,0:T(8,128)} %get-tuple-element.5) | copy-start | bytes 786436

commit v3 on v2

--- a/solution.py
+++ b/solution.py
@@ -23,7 +23,7 @@
 
 def kernel(users, feats, one_ref, two_ref, partner_ref, g1_ref, g2_ref,
            views, partners, part, rs, colst, rowst, stage, coup, cols,
-           local_sem, view_recv, line_send, group_send, partner_send, partner_recv,
+           local_sem, view_recv, line_send, straight_send, beside_send, group_send, partner_send, partner_recv,
            rs_send, rs_recv, col_send, col_recv, row_send, row_recv,
            coup_send, coup_recv, turn_send, turn_recv, cols_send, cols_recv):
     rows, width = one_ref.shape
@@ -40,9 +40,9 @@
 
     loads = [pltpu.make_async_copy(ref, views.at[v, u], local_sem.at[v])
              for v, ref in enumerate((two_ref, one_ref))]
+    loads.append(pltpu.make_async_copy(partner_ref, partners.at[y], local_sem.at[2]))
     for load in loads:
         load.start()
-    partners[y] = partner_ref[...]
 
     def line_at(k):
         return lax.rem(z + k, length)
@@ -63,18 +63,30 @@
             src_ref=src, dst_ref=dst, send_sem=send, recv_sem=recv,
             device_id=(to_z * group + to_y, to_f), device_id_type=MESH)
 
-    def along(v, src, step):
+    def half(v, b, h):
+        return views.at[v, b, pl.ds(h * (rows // 2), rows // 2)]
+
+    def along(src, step, h):
         b = src * group + y
-        return remote(views.at[v, b], views.at[v, b], line_send.at[v, src, (step + 1) // 2],
-                      view_recv.at[v, b], z + step, y, f)
+        return remote(half(0, b, h), half(0, b, h), line_send.at[src, (step + 1) // 2, h],
+                      view_recv.at[0, b, h], z + step, y, f)
+
+    def straight(k):
+        return remote(views.at[1, u], views.at[1, u], straight_send.at[k - 1],
+                      view_recv.at[1, u, 0], line_at(k), y, f)
+
+    def beside(step, k):
+        b = z * group + lax.rem(y + k, group)
+        return remote(views.at[1, b], views.at[1, b], beside_send.at[(step + 1) // 2, k - 1],
+                      view_recv.at[1, b, 0], z + step, y, f)
 
     def across(v, src, k):
         b = src * group + y
         return remote(views.at[v, b], views.at[v, b], group_send.at[v, src, k - 1],
-                      view_recv.at[v, b], z, lax.rem(y + k, group), f)
+                      view_recv.at[v, b, 0], z, lax.rem(y + k, group), f)
 
     def arrived(v, b):
-        remote(views.at[v, b], views.at[v, b], line_send.at[v, 0, 0], view_recv.at[v, b], z, y, f).wait_recv()
+        remote(views.at[v, b], views.at[v, b], line_send.at[0, 0, 0], view_recv.at[v, b, 0], z, y, f).wait_recv()
 
     def each_on_line(d, body):
         for step in ((1, -1) if d else (0,)):
@@ -90,26 +102,41 @@
             def _():
                 act(way)
 
-    def pass_on(v, d):
-        def body(src, step):
-            if d:
-                arrived(v, src * group + y)
-            onward(step, lambda way: along(v, src, way).start())
-        each_on_line(d, body)
+    def pass_on(d):
+        for h in range(2):
+            def body(src, step):
+                if d:
+                    along(src, step, h).wait_recv()
+                onward(step, lambda way: along(src, way, h).start())
+            each_on_line(d, body)
+
+    def first_views():
+        for d in range(1, length):
+            each_on_line(d, lambda dst, step: straight(d if step > 0 else length - d).start())
+        onward(0, lambda way: [beside(way, k).start() for k in range(1, group)])
 
     def cross(v, d):
         def body(src, step):
-            for k in range(1, group):
-                across(v, src, k).start()
+            if v and d:
+                arrived(1, src * group + y)
+            if v == 0 or d != 1:
+                for k in range(1, group):
+                    across(v, src, k).start()
         each_on_line(d, body)
 
-    def sent(v):
+    def sent():
         for d in range(length):
             def body(src, step):
-                onward(step, lambda way: along(v, src, way).wait_send())
-                for k in range(1, group):
-                    across(v, src, k).wait_send()
+                for h in range(2):
+                    onward(step, lambda way: along(src, way, h).wait_send())
+                for v in range(2):
+                    if v == 0 or d != 1:
+                        for k in range(1, group):
+                            across(v, src, k).wait_send()
             each_on_line(d, body)
+        for k in range(1, length):
+            straight(k).wait_send()
+        onward(0, lambda way: [beside(way, k).wait_send() for k in range(1, group)])
 
     def crossed(v):
         def one(src, carry):
@@ -137,9 +164,10 @@
         each_on_line(d, body)
 
     loads[0].wait()
-    pass_on(0, 0)
+    pass_on(0)
     loads[1].wait()
     cross(1, 0)
+    loads[2].wait()
     for k in range(1, group):
         partner_copy(k).start()
     cross(0, 0)
@@ -147,9 +175,9 @@
         arrived(1, z * group + lax.rem(y + k, group))
     score(0)
     for d in range(1, length):
-        pass_on(0, d)
-        if d == length - 1:
-            pass_on(1, 0)
+        pass_on(d)
+        if d == max(length - 2, 1):
+            first_views()
         score(d)
         cross(0, d)
 
@@ -183,8 +211,6 @@
         col_copy(k).start()
     for p in range(1, plane):
         row_copy(p).start()
-    pass_on(1, 1)
-    cross(1, 1)
     for k in range(1, group):
         partner_copy(k).wait_recv()
     for p in range(1, plane):
@@ -225,15 +251,12 @@
         coup_copy(p).start()
     coup[:, y, mine, :] = stage[y]
     cols[pl.ds(z * group, group), mine, :] = stage[:, z]
-    pass_on(1, 2)
-    cross(1, 2)
+    for d in range(2, length):
+        cross(1, d)
     for k in range(1, length):
         turn_copy(k).wait_recv()
     for k in range(1, feats):
         cols_copy(k).start()
-    for d in range(3, length):
-        pass_on(1, d)
-        cross(1, d)
 
     def summed(out_ref, term):
         chunk = math.gcd(users, 8)
@@ -259,6 +282,8 @@
         coup_copy(p).wait_recv()
     crossed(0)
     summed(g1_ref, one_term)
+
+    cross(1, 1)
 
     def late(src, carry):
         @pl.when(src != z)
@@ -271,8 +296,7 @@
         cols_copy(k).wait_recv()
     summed(g2_ref, two_term)
 
-    sent(0)
-    sent(1)
+    sent()
 
     def rs_sent(src, carry):
         for k in range(1, feats):
@@ -289,6 +313,15 @@
         coup_copy(p).wait_send()
     for k in range(1, feats):
         cols_copy(k).wait_send()
+
+
+def hand_out(one_ref, two_ref, one_out, two_out, sems):
+    copies = [pltpu.make_async_copy(one_ref, one_out, sems.at[0]),
+              pltpu.make_async_copy(two_ref, two_out, sems.at[1])]
+    for copy in copies:
+        copy.start()
+    for copy in copies:
+        copy.wait()
 
 
 def on_device(users, feats, view_one, view_two, partner):
@@ -302,10 +335,10 @@
     anywhere = pl.BlockSpec(memory_space=pl.ANY)
     dma = pltpu.SemaphoreType.DMA
     f32, bf16 = jnp.float32, jnp.bfloat16
-    return pl.pallas_call(
+    grads = pl.pallas_call(
         functools.partial(kernel, users, feats),
         out_shape=(out, out),
-        in_specs=[anywhere, anywhere, vmem],
+        in_specs=[pl.BlockSpec(memory_space=pltpu.HBM)] * 3,
         out_specs=(vmem, vmem),
         scratch_shapes=[
             pltpu.VMEM((2, users, rows, width), bf16),
@@ -317,9 +350,11 @@
             pltpu.VMEM((group, length, quarter, rows), bf16),
             pltpu.VMEM((length, group, rows, rows), bf16),
             pltpu.VMEM((users, rows, rows), bf16),
-            dma((2,)),
-            dma((2, users)),
-            dma((2, length, 2)),
+            dma((3,)),
+            dma((2, users, 2)),
+            dma((length, 2, 2)),
+            dma((length - 1,)),
+            dma((2, group - 1)),
             dma((2, length, group - 1)),
             dma((group - 1,)), dma((group - 1,)),
             dma((feats - 1, length)), dma((feats - 1, length)),
@@ -330,11 +365,18 @@
             dma((feats - 1,)), dma((feats - 1,)),
         ],
         compiler_params=pltpu.CompilerParams(
-            collective_id=0, has_side_effects=True, vmem_limit_bytes=60 * 1024 * 1024),
+            collective_id=0, has_side_effects=True, vmem_limit_bytes=min(60, 8 + users) * 1024 * 1024),
         cost_estimate=pl.CostEstimate(
             flops=6 * users * rows * rows * width, bytes_accessed=16 * rows * width,
             transcendentals=4 * users * quarter * rows),
     )(view_one, view_two, partner.reshape(1, rows))
+    return pl.pallas_call(
+        hand_out,
+        out_shape=(out, out),
+        in_specs=[anywhere, anywhere],
+        out_specs=(anywhere, anywhere),
+        scratch_shapes=[dma((2,))],
+    )(*grads)
 
 
 def solution(mesh):

time: 43.2 us -> 62.7 us (1.45)
  Pallas kernels: 40 us -> 58.1 us
  local copies, waits for them, and re-layouts: 2.42 us -> 3.84 us
    pallas_call x0 -> x1, Pallas kernels: none -> 17 us  [on_device(): pl.pallas_call(hand_out, out_shape=(out, out), in_specs=[anywhere, anywhe...]
    unnamed x4 -> x10, local copies, waits for them, and re-layouts: 2.42 us -> 3.84 us
    pallas_call x1, Pallas kernels: 40 us -> 41.1 us  [on_device(): pl.pallas_call(functools.partial(kernel, users, feats), out_shape=(out, o...]
where the time goes in v3:
time: 62.7 us; the launch traced here: 62.6 us
  Pallas kernels  58.1 us (93%)
  local copies, waits for them, and re-layouts  3.84 us (6%)
  between operations  0.66 us (1%)
    pallas_call x1, Pallas kernels, on_device(): pl.pallas_call(functools.partial(kernel, users, feats), out_shape=(out, o...  41.1 us
    pallas_call x1, Pallas kernels, on_device(): pl.pallas_call(hand_out, out_shape=(out, out), in_specs=[anywhere, anywhe...  17 us
    unnamed x10, local copies, waits for them, and re-layouts  3.84 us

profile of v3, /device:TPU:0, one launch (start us, length us, event | category | flops | bytes accessed | tf_op | source)
XLA Modules:
  0.0 62.6 jit_solution(3166185465615001897)
XLA Ops:
  0.6 0.0 copy-start.4
  0.6 0.6 %copy-done.4 = s32[128]{0:T(128)S(1)} copy-done((s32[128]{0:T(128)S(1)}, s32[128]{0:T(128)}, u32[]{:S(2)}) %copy-start.4) | copy-done | bytes 536
  1.3 0.0 copy-start.2
  1.3 0.9 %copy-done.2 = bf16[128,512]{1,0:T(8,128)(2,1)S(1)} copy-done((bf16[128,512]{1,0:T(8,128)(2,1)S(1)}, bf16[128,512]{1,0:T(8,128)(2,1)}, u32[]{:S(2)}) %copy-start.2) | copy-done | bytes 131096
  2.2 0.0 copy-start.3
  2.2 0.9 %copy-done.3 = bf16[128,512]{1,0:T(8,128)(2,1)S(1)} copy-done((bf16[128,512]{1,0:T(8,128)(2,1)S(1)}, bf16[128,512]{1,0:T(8,128)(2,1)}, u32[]{:S(2)}) %copy-start.3) | copy-done | bytes 131096
  3.1 41.1 %shard_map.50 = (f32[128,512]{1,0:T(8,128)S(1)}, f32[128,512]{1,0:T(8,128)S(1)}) custom-call(bf16[128,512]{1,0:T(8,128)(2,1)S(1)} %copy-done.2, bf16[128,512]{1,0:T(8,128)(2,1)S(1)} %copy-done.3, s32[1,128]{1,0:T(1,128)S(1)} %bitcast.1), custom_call_target="tpu_custom_call" | custom-call | flops 402653184 | bytes 1048576 | tf_op jit(solution)/shard_map/pallas_call | solution.py:338
  44.2 0.0 copy-start
  44.2 0.7 %copy-done = f32[128,512]{1,0:T(8,128)} copy-done((f32[128,512]{1,0:T(8,128)}, f32[128,512]{1,0:T(8,128)S(1)}, u32[]{:S(2)}) %copy-start) | copy-done | bytes 262168
  44.9 0.0 copy-start.1
  44.9 0.7 %copy-done.1 = f32[128,512]{1,0:T(8,128)} copy-done((f32[128,512]{1,0:T(8,128)}, f32[128,512]{1,0:T(8,128)S(1)}, u32[]{:S(2)}) %copy-start.1) | copy-done | bytes 262168
  45.6 17.0 %shard_map.51 = (f32[128,512]{1,0:T(8,128)}, f32[128,512]{1,0:T(8,128)}) custom-call(f32[128,512]{1,0:T(8,128)} %copy-done, f32[128,512]{1,0:T(8,128)} %copy-done.1), custom_call_target="tpu_custom_call" | custom-call | tf_op jit(solution)/shard_map/pallas_call | solution.py:373
Async XLA Ops:
  0.6 0.7 %copy-start.4 = (s32[128]{0:T(128)S(1)}, s32[128]{0:T(128)}, u32[]{:S(2)}) copy-start(s32[128]{0:T(128)} %param.5) | copy-start | bytes 1540
  1.3 0.9 %copy-start.2 = (bf16[128,512]{1,0:T(8,128)(2,1)S(1)}, bf16[128,512]{1,0:T(8,128)(2,1)}, u32[]{:S(2)}) copy-start(bf16[128,512]{1,0:T(8,128)(2,1)} %one_ref.1) | copy-start | bytes 393220
  2.2 0.9 %copy-start.3 = (bf16[128,512]{1,0:T(8,128)(2,1)S(1)}, bf16[128,512]{1,0:T(8,128)(2,1)}, u32[]{:S(2)}) copy-start(bf16[128,512]{1,0:T(8,128)(2,1)} %two_ref.1) | copy-start | bytes 393220
  44.2 0.7 %copy-start = (f32[128,512]{1,0:T(8,128)}, f32[128,512]{1,0:T(8,128)S(1)}, u32[]{:S(2)}) copy-start(f32[128,512]{1,0:T(8,128)S(1)} %get-tuple-element.4.one_ref) | copy-start | bytes 786436
  44.9 0.7 %copy-start.1 = (f32[128,512]{1,0:T(8,128)}, f32[128,512]{1,0:T(8,128)S(1)}, u32[]{:S(2)}) copy-start(f32[128,512]{1,0:T(8,128)S(1)} %get-tuple-element.5.two_ref) | copy-start | bytes 786436

commit v4 on v3

--- a/solution.py
+++ b/solution.py
@@ -9,6 +9,7 @@
 from jax.sharding import PartitionSpec as P
 
 D = 2048
+VMEM_BYTES = 60 * 1024 * 1024
 MESH = pl.DeviceIdType.MESH
 NT = (((1,), (1,)), ((), ()))
 TN = (((0,), (0,)), ((), ()))
@@ -71,9 +72,9 @@
         return remote(half(0, b, h), half(0, b, h), line_send.at[src, (step + 1) // 2, h],
                       view_recv.at[0, b, h], z + step, y, f)
 
-    def straight(k):
-        return remote(views.at[1, u], views.at[1, u], straight_send.at[k - 1],
-                      view_recv.at[1, u, 0], line_at(k), y, f)
+    def straight(v, k):
+        return remote(views.at[v, u], views.at[v, u], straight_send.at[v, k - 1],
+                      view_recv.at[v, u, 0], line_at(k), y, f)
 
     def beside(step, k):
         b = z * group + lax.rem(y + k, group)
@@ -102,17 +103,27 @@
             def _():
                 act(way)
 
+    def far(v, d, act):
+        each_on_line(d, lambda dst, step: act(straight(v, d if step > 0 else length - d)))
+
     def pass_on(d):
         for h in range(2):
             def body(src, step):
                 if d:
                     along(src, step, h).wait_recv()
-                onward(step, lambda way: along(src, way, h).start())
-            each_on_line(d, body)
+                if d < 2:
+                    onward(step, lambda way: along(src, way, h).start())
+            if d < 3:
+                each_on_line(d, body)
+        if d == 0:
+            for reach in range(length - 1, 2, -1):
+                far(0, reach, lambda copy: copy.start())
+        if d > 2:
+            each_on_line(d, lambda src, step: arrived(0, src * group + y))
 
     def first_views():
-        for d in range(1, length):
-            each_on_line(d, lambda dst, step: straight(d if step > 0 else length - d).start())
+        for d in range(length - 1, 0, -1):
+            far(1, d, lambda copy: copy.start())
         onward(0, lambda way: [beside(way, k).start() for k in range(1, group)])
 
     def cross(v, d):
@@ -127,15 +138,17 @@
     def sent():
         for d in range(length):
             def body(src, step):
-                for h in range(2):
+                for h in range(2 if d < 2 else 0):
                     onward(step, lambda way: along(src, way, h).wait_send())
                 for v in range(2):
                     if v == 0 or d != 1:
                         for k in range(1, group):
                             across(v, src, k).wait_send()
             each_on_line(d, body)
-        for k in range(1, length):
-            straight(k).wait_send()
+        for d in range(1, length):
+            far(1, d, lambda copy: copy.wait_send())
+        for d in range(3, length):
+            far(0, d, lambda copy: copy.wait_send())
         onward(0, lambda way: [beside(way, k).wait_send() for k in range(1, group)])
 
     def crossed(v):
@@ -176,7 +189,7 @@
     score(0)
     for d in range(1, length):
         pass_on(d)
-        if d == max(length - 2, 1):
+        if d == 1:
             first_views()
         score(d)
         cross(0, d)
@@ -315,13 +328,19 @@
         cols_copy(k).wait_send()
 
 
-def hand_out(one_ref, two_ref, one_out, two_out, sems):
-    copies = [pltpu.make_async_copy(one_ref, one_out, sems.at[0]),
-              pltpu.make_async_copy(two_ref, two_out, sems.at[1])]
-    for copy in copies:
+def hand_out(one_ref, two_ref, one_out, two_out, held, come, go):
+    rows = held.shape[1] // 2
+    parts = [(v, h, ref.at[pl.ds(h * rows, rows)], out.at[pl.ds(h * rows, rows)], held.at[v, pl.ds(h * rows, rows)])
+             for v, (ref, out) in enumerate(((one_ref, one_out), (two_ref, two_out))) for h in range(2)]
+    ins = [pltpu.make_async_copy(src, slot, come.at[v, h]) for v, h, src, _, slot in parts]
+    outs = [pltpu.make_async_copy(slot, dst, go.at[v, h]) for v, h, _, dst, slot in parts]
+    for copy in ins:
         copy.start()
-    for copy in copies:
+    for copy, out in zip(ins, outs):
         copy.wait()
+        out.start()
+    for out in outs:
+        out.wait()
 
 
 def on_device(users, feats, view_one, view_two, partner):
@@ -338,7 +357,7 @@
     grads = pl.pallas_call(
         functools.partial(kernel, users, feats),
         out_shape=(out, out),
-        in_specs=[pl.BlockSpec(memory_space=pltpu.HBM)] * 3,
+        in_specs=[anywhere] * 3,
         out_specs=(vmem, vmem),
         scratch_shapes=[
             pltpu.VMEM((2, users, rows, width), bf16),
@@ -353,7 +372,7 @@
             dma((3,)),
             dma((2, users, 2)),
             dma((length, 2, 2)),
-            dma((length - 1,)),
+            dma((2, length - 1)),
             dma((2, group - 1)),
             dma((2, length, group - 1)),
             dma((group - 1,)), dma((group - 1,)),
@@ -365,7 +384,7 @@
             dma((feats - 1,)), dma((feats - 1,)),
         ],
         compiler_params=pltpu.CompilerParams(
-            collective_id=0, has_side_effects=True, vmem_limit_bytes=min(60, 8 + users) * 1024 * 1024),
+            collective_id=0, has_side_effects=True, vmem_limit_bytes=VMEM_BYTES),
         cost_estimate=pl.CostEstimate(
             flops=6 * users * rows * rows * width, bytes_accessed=16 * rows * width,
             transcendentals=4 * users * quarter * rows),
@@ -375,7 +394,8 @@
         out_shape=(out, out),
         in_specs=[anywhere, anywhere],
         out_specs=(anywhere, anywhere),
-        scratch_shapes=[dma((2,))],
+        scratch_shapes=[pltpu.VMEM((2, rows, width), f32), dma((2, 2)), dma((2, 2))],
+        compiler_params=pltpu.CompilerParams(vmem_limit_bytes=VMEM_BYTES),
     )(*grads)
 
 

time: 62.7 us -> 46.1 us (0.74)
  Pallas kernels: 58.1 us -> 45.3 us
  local copies, waits for them, and re-layouts: 3.84 us -> 0 us
    pallas_call x1, Pallas kernels: 17 us -> 1.82 us  [on_device(): pl.pallas_call(hand_out, out_shape=(out, out), in_specs=[anywhere, anywhe...]
    unnamed x10 -> x0, local copies, waits for them, and re-layouts: 3.84 us -> none
    pallas_call x1, Pallas kernels: 41.1 us -> 43.5 us  [on_device(): pl.pallas_call(functools.partial(kernel, users, feats), out_shape=(out, o...]
where the time goes in v4:
time: 46.1 us; the launch traced here: 45.9 us
  Pallas kernels  45.3 us (98%)
  between operations  0.64 us (1%)
    pallas_call x1, Pallas kernels, on_device(): pl.pallas_call(functools.partial(kernel, users, feats), out_shape=(out, o...  43.5 us
    pallas_call x1, Pallas kernels, on_device(): pl.pallas_call(hand_out, out_shape=(out, out), in_specs=[anywhere, anywhe...  1.82 us

profile of v4, /device:TPU:0, one launch (start us, length us, event | category | flops | bytes accessed | tf_op | source)
XLA Modules:
  0.0 45.9 jit_solution(9499814461657927751)
XLA Ops:
  0.6 43.5 %shard_map.50 = (f32[128,512]{1,0:T(8,128)}, f32[128,512]{1,0:T(8,128)}) custom-call(bf16[128,512]{1,0:T(8,128)(2,1)} %one_ref.1, bf16[128,512]{1,0:T(8,128)(2,1)} %two_ref.1, s32[1,128]{1,0:T(1,128)} %bitcast.1), custom_call_target="tpu_custom_call" | custom-call | flops 402653184 | bytes 1048576 | tf_op jit(solution)/shard_map/pallas_call | solution.py:357
  44.1 1.8 %shard_map.51 = (f32[128,512]{1,0:T(8,128)}, f32[128,512]{1,0:T(8,128)}) custom-call(f32[128,512]{1,0:T(8,128)} %get-tuple-element.4.one_ref, f32[128,512]{1,0:T(8,128)} %get-tuple-element.5.two_ref), custom_call_target="tpu_custom_call" | custom-call | tf_op jit(solution)/shard_map/pallas_call | solution.py:392

commit v5 on v4

--- a/solution.py
+++ b/solution.py
@@ -24,7 +24,7 @@
 
 def kernel(users, feats, one_ref, two_ref, partner_ref, g1_ref, g2_ref,
            views, partners, part, rs, colst, rowst, stage, coup, cols,
-           local_sem, view_recv, line_send, straight_send, beside_send, group_send, partner_send, partner_recv,
+           local_sem, view_recv, line_send, straight_send, group_send, partner_send, partner_recv,
            rs_send, rs_recv, col_send, col_recv, row_send, row_recv,
            coup_send, coup_recv, turn_send, turn_recv, cols_send, cols_recv):
     rows, width = one_ref.shape
@@ -75,11 +75,6 @@
     def straight(v, k):
         return remote(views.at[v, u], views.at[v, u], straight_send.at[v, k - 1],
                       view_recv.at[v, u, 0], line_at(k), y, f)
-
-    def beside(step, k):
-        b = z * group + lax.rem(y + k, group)
-        return remote(views.at[1, b], views.at[1, b], beside_send.at[(step + 1) // 2, k - 1],
-                      view_recv.at[1, b, 0], z + step, y, f)
 
     def across(v, src, k):
         b = src * group + y
@@ -121,18 +116,12 @@
         if d > 2:
             each_on_line(d, lambda src, step: arrived(0, src * group + y))
 
-    def first_views():
-        for d in range(length - 1, 0, -1):
-            far(1, d, lambda copy: copy.start())
-        onward(0, lambda way: [beside(way, k).start() for k in range(1, group)])
-
     def cross(v, d):
         def body(src, step):
             if v and d:
                 arrived(1, src * group + y)
-            if v == 0 or d != 1:
-                for k in range(1, group):
-                    across(v, src, k).start()
+            for k in range(1, group):
+                across(v, src, k).start()
         each_on_line(d, body)
 
     def sent():
@@ -141,15 +130,13 @@
                 for h in range(2 if d < 2 else 0):
                     onward(step, lambda way: along(src, way, h).wait_send())
                 for v in range(2):
-                    if v == 0 or d != 1:
-                        for k in range(1, group):
-                            across(v, src, k).wait_send()
+                    for k in range(1, group):
+                        across(v, src, k).wait_send()
             each_on_line(d, body)
         for d in range(1, length):
             far(1, d, lambda copy: copy.wait_send())
         for d in range(3, length):
             far(0, d, lambda copy: copy.wait_send())
-        onward(0, lambda way: [beside(way, k).wait_send() for k in range(1, group)])
 
     def crossed(v):
         def one(src, carry):
@@ -189,8 +176,9 @@
     score(0)
     for d in range(1, length):
         pass_on(d)
-        if d == 1:
-            first_views()
+        if d == length - 1:
+            for reach in range(1, length):
+                far(1, reach, lambda copy: copy.start())
         score(d)
         cross(0, d)
 
@@ -224,6 +212,7 @@
         col_copy(k).start()
     for p in range(1, plane):
         row_copy(p).start()
+    cross(1, 1)
     for k in range(1, group):
         partner_copy(k).wait_recv()
     for p in range(1, plane):
@@ -264,12 +253,13 @@
         coup_copy(p).start()
     coup[:, y, mine, :] = stage[y]
     cols[pl.ds(z * group, group), mine, :] = stage[:, z]
-    for d in range(2, length):
-        cross(1, d)
+    cross(1, 2)
     for k in range(1, length):
         turn_copy(k).wait_recv()
     for k in range(1, feats):
         cols_copy(k).start()
+    for d in range(3, length):
+        cross(1, d)
 
     def summed(out_ref, term):
         chunk = math.gcd(users, 8)
@@ -295,8 +285,6 @@
         coup_copy(p).wait_recv()
     crossed(0)
     summed(g1_ref, one_term)
-
-    cross(1, 1)
 
     def late(src, carry):
         @pl.when(src != z)
@@ -373,7 +361,6 @@
             dma((2, users, 2)),
             dma((length, 2, 2)),
             dma((2, length - 1)),
-            dma((2, group - 1)),
             dma((2, length, group - 1)),
             dma((group - 1,)), dma((group - 1,)),
             dma((feats - 1, length)), dma((feats - 1, length)),

time: 46.1 us -> 43.9 us (0.952)
  Pallas kernels: 45.3 us -> 43.1 us
    pallas_call x1, Pallas kernels: 43.5 us -> 41.3 us  [on_device(): pl.pallas_call(functools.partial(kernel, users, feats), out_shape=(out, o...]
where the time goes in v5:
time: 43.9 us; the launch traced here: 43.8 us
  Pallas kernels  43.1 us (98%)
  between operations  0.64 us (1%)
    pallas_call x1, Pallas kernels, on_device(): pl.pallas_call(functools.partial(kernel, users, feats), out_shape=(out, o...  41.3 us
    pallas_call x1, Pallas kernels, on_device(): pl.pallas_call(hand_out, out_shape=(out, out), in_specs=[anywhere, anywhe...  1.82 us

profile of v5, /device:TPU:0, one launch (start us, length us, event | category | flops | bytes accessed | tf_op | source)
XLA Modules:
  0.0 43.8 jit_solution(8061644227314377183)
XLA Ops:
  0.6 41.3 %shard_map.50 = (f32[128,512]{1,0:T(8,128)}, f32[128,512]{1,0:T(8,128)}) custom-call(bf16[128,512]{1,0:T(8,128)(2,1)} %one_ref.1, bf16[128,512]{1,0:T(8,128)(2,1)} %two_ref.1, s32[1,128]{1,0:T(1,128)} %bitcast.1), custom_call_target="tpu_custom_call" | custom-call | flops 402653184 | bytes 1048576 | tf_op jit(solution)/shard_map/pallas_call | solution.py:345
  41.9 1.8 %shard_map.51 = (f32[128,512]{1,0:T(8,128)}, f32[128,512]{1,0:T(8,128)}) custom-call(f32[128,512]{1,0:T(8,128)} %get-tuple-element.4.one_ref, f32[128,512]{1,0:T(8,128)} %get-tuple-element.5.two_ref), custom_call_target="tpu_custom_call" | custom-call | tf_op jit(solution)/shard_map/pallas_call | solution.py:379

commit v6 on v5

--- a/solution.py
+++ b/solution.py
@@ -10,6 +10,7 @@
 
 D = 2048
 VMEM_BYTES = 60 * 1024 * 1024
+PIECES = (2, 1)
 MESH = pl.DeviceIdType.MESH
 NT = (((1,), (1,)), ((), ()))
 TN = (((0,), (0,)), ((), ()))
@@ -24,7 +25,7 @@
 
 def kernel(users, feats, one_ref, two_ref, partner_ref, g1_ref, g2_ref,
            views, partners, part, rs, colst, rowst, stage, coup, cols,
-           local_sem, view_recv, line_send, straight_send, group_send, partner_send, partner_recv,
+           local_sem, view_recv, line_send, group_send, partner_send, partner_recv,
            rs_send, rs_recv, col_send, col_recv, row_send, row_recv,
            coup_send, coup_recv, turn_send, turn_recv, cols_send, cols_recv):
     rows, width = one_ref.shape
@@ -64,17 +65,14 @@
             src_ref=src, dst_ref=dst, send_sem=send, recv_sem=recv,
             device_id=(to_z * group + to_y, to_f), device_id_type=MESH)
 
-    def half(v, b, h):
-        return views.at[v, b, pl.ds(h * (rows // 2), rows // 2)]
-
-    def along(src, step, h):
+    def piece(v, b, h):
+        size = rows // PIECES[v]
+        return views.at[v, b, pl.ds(h * size, size)]
+
+    def along(v, src, step, h):
         b = src * group + y
-        return remote(half(0, b, h), half(0, b, h), line_send.at[src, (step + 1) // 2, h],
-                      view_recv.at[0, b, h], z + step, y, f)
-
-    def straight(v, k):
-        return remote(views.at[v, u], views.at[v, u], straight_send.at[v, k - 1],
-                      view_recv.at[v, u, 0], line_at(k), y, f)
+        return remote(piece(v, b, h), piece(v, b, h), line_send.at[v, src, (step + 1) // 2, h],
+                      view_recv.at[v, b, h], z + step, y, f)
 
     def across(v, src, k):
         b = src * group + y
@@ -82,7 +80,7 @@
                       view_recv.at[v, b, 0], z, lax.rem(y + k, group), f)
 
     def arrived(v, b):
-        remote(views.at[v, b], views.at[v, b], line_send.at[0, 0, 0], view_recv.at[v, b, 0], z, y, f).wait_recv()
+        remote(views.at[v, b], views.at[v, b], line_send.at[0, 0, 0, 0], view_recv.at[v, b, 0], z, y, f).wait_recv()
 
     def each_on_line(d, body):
         for step in ((1, -1) if d else (0,)):
@@ -98,45 +96,28 @@
             def _():
                 act(way)
 
-    def far(v, d, act):
-        each_on_line(d, lambda dst, step: act(straight(v, d if step > 0 else length - d)))
-
-    def pass_on(d):
-        for h in range(2):
+    def pass_on(v, d):
+        for h in range(PIECES[v]):
             def body(src, step):
                 if d:
-                    along(src, step, h).wait_recv()
-                if d < 2:
-                    onward(step, lambda way: along(src, way, h).start())
-            if d < 3:
-                each_on_line(d, body)
-        if d == 0:
-            for reach in range(length - 1, 2, -1):
-                far(0, reach, lambda copy: copy.start())
-        if d > 2:
-            each_on_line(d, lambda src, step: arrived(0, src * group + y))
+                    along(v, src, step, h).wait_recv()
+                onward(step, lambda way: along(v, src, way, h).start())
+            each_on_line(d, body)
 
     def cross(v, d):
         def body(src, step):
-            if v and d:
-                arrived(1, src * group + y)
             for k in range(1, group):
                 across(v, src, k).start()
         each_on_line(d, body)
 
-    def sent():
+    def sent(v):
         for d in range(length):
             def body(src, step):
-                for h in range(2 if d < 2 else 0):
-                    onward(step, lambda way: along(src, way, h).wait_send())
-                for v in range(2):
-                    for k in range(1, group):
-                        across(v, src, k).wait_send()
+                for h in range(PIECES[v]):
+                    onward(step, lambda way: along(v, src, way, h).wait_send())
+                for k in range(1, group):
+                    across(v, src, k).wait_send()
             each_on_line(d, body)
-        for d in range(1, length):
-            far(1, d, lambda copy: copy.wait_send())
-        for d in range(3, length):
-            far(0, d, lambda copy: copy.wait_send())
 
     def crossed(v):
         def one(src, carry):
@@ -164,7 +145,7 @@
         each_on_line(d, body)
 
     loads[0].wait()
-    pass_on(0)
+    pass_on(0, 0)
     loads[1].wait()
     cross(1, 0)
     loads[2].wait()
@@ -175,12 +156,13 @@
         arrived(1, z * group + lax.rem(y + k, group))
     score(0)
     for d in range(1, length):
-        pass_on(d)
-        if d == length - 1:
-            for reach in range(1, length):
-                far(1, reach, lambda copy: copy.start())
+        pass_on(0, d)
+        if d == max(length - 2, 1):
+            pass_on(1, 0)
         score(d)
         cross(0, d)
+    pass_on(1, 1)
+    cross(1, 1)
 
     def rs_wait(src, carry):
         for k in range(1, feats):
@@ -212,7 +194,8 @@
         col_copy(k).start()
     for p in range(1, plane):
         row_copy(p).start()
-    cross(1, 1)
+    pass_on(1, 2)
+    cross(1, 2)
     for k in range(1, group):
         partner_copy(k).wait_recv()
     for p in range(1, plane):
@@ -253,13 +236,13 @@
         coup_copy(p).start()
     coup[:, y, mine, :] = stage[y]
     cols[pl.ds(z * group, group), mine, :] = stage[:, z]
-    cross(1, 2)
+    for d in range(3, length):
+        pass_on(1, d)
+        cross(1, d)
     for k in range(1, length):
         turn_copy(k).wait_recv()
     for k in range(1, feats):
         cols_copy(k).start()
-    for d in range(3, length):
-        cross(1, d)
 
     def summed(out_ref, term):
         chunk = math.gcd(users, 8)
@@ -297,7 +280,8 @@
         cols_copy(k).wait_recv()
     summed(g2_ref, two_term)
 
-    sent()
+    sent(0)
+    sent(1)
 
     def rs_sent(src, carry):
         for k in range(1, feats):
@@ -359,8 +343,7 @@
             pltpu.VMEM((users, rows, rows), bf16),
             dma((3,)),
             dma((2, users, 2)),
-            dma((length, 2, 2)),
-            dma((2, length - 1)),
+            dma((2, length, 2, 2)),
             dma((2, length, group - 1)),
             dma((group - 1,)), dma((group - 1,)),
             dma((feats - 1, length)), dma((feats - 1, length)),

time: 43.9 us -> 40 us (0.911)
  Pallas kernels: 43.1 us -> 39.2 us
    pallas_call x1, Pallas kernels: 41.3 us -> 37.4 us  [on_device(): pl.pallas_call(functools.partial(kernel, users, feats), out_shape=(out, o...]
where the time goes in v6:
time: 40 us; the launch traced here: 39.9 us
  Pallas kernels  39.2 us (98%)
  between operations  0.64 us (2%)
    pallas_call x1, Pallas kernels, on_device(): pl.pallas_call(functools.partial(kernel, users, feats), out_shape=(out, o...  37.4 us
    pallas_call x1, Pallas kernels, on_device(): pl.pallas_call(hand_out, out_shape=(out, out), in_specs=[anywhere, anywhe...  1.82 us

profile of v6, /device:TPU:0, one launch (start us, length us, event | category | flops | bytes accessed | tf_op | source)
XLA Modules:
  0.0 39.9 jit_solution(14702881193632977582)
XLA Ops:
  0.6 37.4 %shard_map.50 = (f32[128,512]{1,0:T(8,128)}, f32[128,512]{1,0:T(8,128)}) custom-call(bf16[128,512]{1,0:T(8,128)(2,1)} %one_ref.1, bf16[128,512]{1,0:T(8,128)(2,1)} %two_ref.1, s32[1,128]{1,0:T(1,128)} %bitcast.1), custom_call_target="tpu_custom_call" | custom-call | flops 402653184 | bytes 1048576 | tf_op jit(solution)/shard_map/pallas_call | solution.py:329
  38.1 1.8 %shard_map.51 = (f32[128,512]{1,0:T(8,128)}, f32[128,512]{1,0:T(8,128)}) custom-call(f32[128,512]{1,0:T(8,128)} %get-tuple-element.4.one_ref, f32[128,512]{1,0:T(8,128)} %get-tuple-element.5.two_ref), custom_call_target="tpu_custom_call" | custom-call | tf_op jit(solution)/shard_map/pallas_call | solution.py:362

commit v7 on v6

--- a/solution.py
+++ b/solution.py
@@ -10,7 +10,7 @@
 
 D = 2048
 VMEM_BYTES = 60 * 1024 * 1024
-PIECES = (2, 1)
+PIECES = 2
 MESH = pl.DeviceIdType.MESH
 NT = (((1,), (1,)), ((), ()))
 TN = (((0,), (0,)), ((), ()))
@@ -23,9 +23,9 @@
     return length
 
 
-def kernel(users, feats, one_ref, two_ref, partner_ref, g1_ref, g2_ref,
-           views, partners, part, rs, colst, rowst, stage, coup, cols,
-           local_sem, view_recv, line_send, group_send, partner_send, partner_recv,
+def kernel(users, feats, one_ref, two_ref, partner_ref, g1_out, g2_out,
+           views, partners, part, rs, colst, rowst, stage, coup, cols, g1_ref, g2_ref,
+           out_sem, local_sem, view_recv, line_send, group_send, partner_send, partner_recv,
            rs_send, rs_recv, col_send, col_recv, row_send, row_recv,
            coup_send, coup_recv, turn_send, turn_recv, cols_send, cols_recv):
     rows, width = one_ref.shape
@@ -66,7 +66,7 @@
             device_id=(to_z * group + to_y, to_f), device_id_type=MESH)
 
     def piece(v, b, h):
-        size = rows // PIECES[v]
+        size = rows // PIECES
         return views.at[v, b, pl.ds(h * size, size)]
 
     def along(v, src, step, h):
@@ -74,13 +74,14 @@
         return remote(piece(v, b, h), piece(v, b, h), line_send.at[v, src, (step + 1) // 2, h],
                       view_recv.at[v, b, h], z + step, y, f)
 
-    def across(v, src, k):
+    def across(v, src, k, h):
         b = src * group + y
-        return remote(views.at[v, b], views.at[v, b], group_send.at[v, src, k - 1],
-                      view_recv.at[v, b, 0], z, lax.rem(y + k, group), f)
+        return remote(piece(v, b, h), piece(v, b, h), group_send.at[v, src, k - 1, h],
+                      view_recv.at[v, b, h], z, lax.rem(y + k, group), f)
 
     def arrived(v, b):
-        remote(views.at[v, b], views.at[v, b], line_send.at[0, 0, 0, 0], view_recv.at[v, b, 0], z, y, f).wait_recv()
+        for h in range(PIECES):
+            remote(piece(v, b, h), piece(v, b, h), line_send.at[0, 0, 0, 0], view_recv.at[v, b, h], z, y, f).wait_recv()
 
     def each_on_line(d, body):
         for step in ((1, -1) if d else (0,)):
@@ -97,26 +98,30 @@
                 act(way)
 
     def pass_on(v, d):
-        for h in range(PIECES[v]):
+        for h in range(PIECES):
             def body(src, step):
                 if d:
                     along(v, src, step, h).wait_recv()
                 onward(step, lambda way: along(v, src, way, h).start())
+                if v and d:
+                    for k in range(1, group):
+                        across(v, src, k, h).start()
             each_on_line(d, body)
 
     def cross(v, d):
         def body(src, step):
-            for k in range(1, group):
-                across(v, src, k).start()
+            for h in range(PIECES):
+                for k in range(1, group):
+                    across(v, src, k, h).start()
         each_on_line(d, body)
 
     def sent(v):
         for d in range(length):
             def body(src, step):
-                for h in range(PIECES[v]):
+                for h in range(PIECES):
                     onward(step, lambda way: along(v, src, way, h).wait_send())
-                for k in range(1, group):
-                    across(v, src, k).wait_send()
+                    for k in range(1, group):
+                        across(v, src, k, h).wait_send()
             each_on_line(d, body)
 
     def crossed(v):
@@ -162,7 +167,6 @@
         score(d)
         cross(0, d)
     pass_on(1, 1)
-    cross(1, 1)
 
     def rs_wait(src, carry):
         for k in range(1, feats):
@@ -195,7 +199,6 @@
     for p in range(1, plane):
         row_copy(p).start()
     pass_on(1, 2)
-    cross(1, 2)
     for k in range(1, group):
         partner_copy(k).wait_recv()
     for p in range(1, plane):
@@ -238,7 +241,6 @@
     cols[pl.ds(z * group, group), mine, :] = stage[:, z]
     for d in range(3, length):
         pass_on(1, d)
-        cross(1, d)
     for k in range(1, length):
         turn_copy(k).wait_recv()
     for k in range(1, feats):
@@ -268,6 +270,8 @@
         coup_copy(p).wait_recv()
     crossed(0)
     summed(g1_ref, one_term)
+    leave_one = pltpu.make_async_copy(g1_ref, g1_out, out_sem.at[0])
+    leave_one.start()
 
     def late(src, carry):
         @pl.when(src != z)
@@ -279,6 +283,8 @@
     for k in range(1, feats):
         cols_copy(k).wait_recv()
     summed(g2_ref, two_term)
+    leave_two = pltpu.make_async_copy(g2_ref, g2_out, out_sem.at[1])
+    leave_two.start()
 
     sent(0)
     sent(1)
@@ -298,6 +304,8 @@
         coup_copy(p).wait_send()
     for k in range(1, feats):
         cols_copy(k).wait_send()
+    leave_one.wait()
+    leave_two.wait()
 
 
 def hand_out(one_ref, two_ref, one_out, two_out, held, come, go):
@@ -322,7 +330,6 @@
     group = users // length
     plane = group * feats
     out = jax.ShapeDtypeStruct((rows, width), jnp.float32)
-    vmem = pl.BlockSpec(memory_space=pltpu.VMEM)
     anywhere = pl.BlockSpec(memory_space=pl.ANY)
     dma = pltpu.SemaphoreType.DMA
     f32, bf16 = jnp.float32, jnp.bfloat16
@@ -330,7 +337,7 @@
         functools.partial(kernel, users, feats),
         out_shape=(out, out),
         in_specs=[anywhere] * 3,
-        out_specs=(vmem, vmem),
+        out_specs=(anywhere, anywhere),
         scratch_shapes=[
             pltpu.VMEM((2, users, rows, width), bf16),
             pltpu.VMEM((group, 1, rows), jnp.int32),
@@ -341,10 +348,13 @@
             pltpu.VMEM((group, length, quarter, rows), bf16),
             pltpu.VMEM((length, group, rows, rows), bf16),
             pltpu.VMEM((users, rows, rows), bf16),
+            pltpu.VMEM((rows, width), f32),
+            pltpu.VMEM((rows, width), f32),
+            dma((2,)),
             dma((3,)),
-            dma((2, users, 2)),
-            dma((2, length, 2, 2)),
-            dma((2, length, group - 1)),
+            dma((2, users, PIECES)),
+            dma((2, length, 2, PIECES)),
+            dma((2, length, group - 1, PIECES)),
             dma((group - 1,)), dma((group - 1,)),
             dma((feats - 1, length)), dma((feats - 1, length)),
             dma((length - 1,)), dma((length - 1,)),

time: 40 us -> 40 us (level)
  no operation moved by 1% of the time
where the time goes in v7:
time: 40 us; the launch traced here: 39.8 us
  Pallas kernels  39.2 us (98%)
  between operations  0.64 us (2%)
    pallas_call x1, Pallas kernels, on_device(): pl.pallas_call(functools.partial(kernel, users, feats), out_shape=(out, o...  37.4 us
    pallas_call x1, Pallas kernels, on_device(): pl.pallas_call(hand_out, out_shape=(out, out), in_specs=[anywhere, anywhe...  1.82 us

profile of v7, /device:TPU:0, one launch (start us, length us, event | category | flops | bytes accessed | tf_op | source)
XLA Modules:
  0.0 39.8 jit_solution(16596619308271162194)
XLA Ops:
  0.6 37.4 %shard_map.50 = (f32[128,512]{1,0:T(8,128)}, f32[128,512]{1,0:T(8,128)}) custom-call(bf16[128,512]{1,0:T(8,128)(2,1)} %one_ref.1, bf16[128,512]{1,0:T(8,128)(2,1)} %two_ref.1, s32[1,128]{1,0:T(1,128)} %bitcast.1), custom_call_target="tpu_custom_call" | custom-call | flops 402653184 | bytes 1048576 | tf_op jit(solution)/shard_map/pallas_call | solution.py:336
  38.0 1.8 %shard_map.51 = (f32[128,512]{1,0:T(8,128)}, f32[128,512]{1,0:T(8,128)}) custom-call(f32[128,512]{1,0:T(8,128)} %get-tuple-element.4.one_ref, f32[128,512]{1,0:T(8,128)} %get-tuple-element.5.two_ref), custom_call_target="tpu_custom_call" | custom-call | tf_op jit(solution)/shard_map/pallas_call | solution.py:372

commit v8 on v7

--- a/solution.py
+++ b/solution.py
@@ -239,12 +239,12 @@
         coup_copy(p).start()
     coup[:, y, mine, :] = stage[y]
     cols[pl.ds(z * group, group), mine, :] = stage[:, z]
-    for d in range(3, length):
-        pass_on(1, d)
     for k in range(1, length):
         turn_copy(k).wait_recv()
     for k in range(1, feats):
         cols_copy(k).start()
+    for d in range(3, length):
+        pass_on(1, d)
 
     def summed(out_ref, term):
         chunk = math.gcd(users, 8)

time: 40 us -> 40.4 us (1.010)
    pallas_call x1, Pallas kernels: 37.4 us -> 37.8 us  [on_device(): pl.pallas_call(functools.partial(kernel, users, feats), out_shape=(out, o...]
where the time goes in v8:
time: 40.4 us; the launch traced here: 40.3 us
  Pallas kernels  39.6 us (98%)
  between operations  0.64 us (2%)
    pallas_call x1, Pallas kernels, on_device(): pl.pallas_call(functools.partial(kernel, users, feats), out_shape=(out, o...  37.8 us
    pallas_call x1, Pallas kernels, on_device(): pl.pallas_call(hand_out, out_shape=(out, out), in_specs=[anywhere, anywhe...  1.82 us

profile of v8, /device:TPU:0, one launch (start us, length us, event | category | flops | bytes accessed | tf_op | source)
XLA Modules:
  0.0 40.3 jit_solution(5074793214146783672)
XLA Ops:
  0.6 37.8 %shard_map.50 = (f32[128,512]{1,0:T(8,128)}, f32[128,512]{1,0:T(8,128)}) custom-call(bf16[128,512]{1,0:T(8,128)(2,1)} %one_ref.1, bf16[128,512]{1,0:T(8,128)(2,1)} %two_ref.1, s32[1,128]{1,0:T(1,128)} %bitcast.1), custom_call_target="tpu_custom_call" | custom-call | flops 402653184 | bytes 1048576 | tf_op jit(solution)/shard_map/pallas_call | solution.py:336
  38.4 1.8 %shard_map.51 = (f32[128,512]{1,0:T(8,128)}, f32[128,512]{1,0:T(8,128)}) custom-call(f32[128,512]{1,0:T(8,128)} %get-tuple-element.4.one_ref, f32[128,512]{1,0:T(8,128)} %get-tuple-element.5.two_ref), custom_call_target="tpu_custom_call" | custom-call | tf_op jit(solution)/shard_map/pallas_call | solution.py:372
